TPU v7x, 32 devices: a whole 2x2x4 slice. The times are simulated.
32 devices in a mesh: grp: 2 (over y), row: 4 (over z), col: 2 (over x), rep: 2 (over core).
Axes of the slice: x: 2, y: 2, z: 4, core: 2. Of those that a mesh axis runs over, the one named last changes fastest.
Arguments:
- integrals: bfloat16 [256, 512, 512], P(('grp', 'col'), 'row', 'rep'), parts along dimension 0, may hold values from -6 to 6
- occ_density: bfloat16 [1024, 512], P('grp', 'rep'), parts along dimension 0, may hold values from -0.25 to 0.25
- virt_density: bfloat16 [1024, 512], P('grp'), parts along dimension 0, may hold values from -0.25 to 0.25
- pair_mask: int32 [8, 4], P('grp'), parts along dimension 0, may hold values 0 or 1
- aux_mask: int32 [2, 4], P('grp'), parts along dimension 0, may hold values 0 or 1
Outputs:
- response: float32 [256, 128], P(('grp', 'row', 'rep'), 'col'), parts along dimension 0
There are 2 independent parts, one for each index of `grp`. A program takes and returns all parts, laid end to end along the dimension named above; each array names one. Nothing has to cross between parts.
All inputs are finite; a program needn't handle non-finite values.
Results may differ from a plain program's by a relative error of at most 0.004.
Values may be sent and summed in bfloat16 or wider, within the bound.
A program may use at most 64 MiB of HBM per device.

v0:
```python
import jax
import jax.numpy as jnp
from jax import lax
from jax.sharding import PartitionSpec as P

BLOCK = 128
RI_ATOM = 128
NAO = 512


def one_hot_blocks(first, count, width, groups):
    places = (first + jnp.arange(count, dtype=jnp.int32)) // width
    return (places[:, None] == jnp.arange(groups, dtype=jnp.int32)[None, :]).astype(jnp.float32)


def local(integrals, occ_density, virt_density, pair_mask, aux_mask):
    ri_count, nu_count, mu_count = integrals.shape
    ao_groups = pair_mask.shape[0]
    ri_groups = aux_mask.shape[0]
    pick_nu = one_hot_blocks(lax.axis_index("row") * nu_count, nu_count, BLOCK, ao_groups)
    pick_mu = one_hot_blocks(lax.axis_index("rep") * mu_count, mu_count, BLOCK, ao_groups)
    pick_ri = one_hot_blocks(lax.axis_index("col") * ri_count, ri_count, RI_ATOM, ri_groups)
    pair_float = pair_mask.astype(jnp.float32)
    aux_float = aux_mask.astype(jnp.float32)
    local_pair = jnp.dot(jnp.dot(pick_nu, jnp.transpose(pair_float)), jnp.transpose(pick_mu))
    local_aux = jnp.dot(jnp.dot(pick_ri, aux_float), jnp.transpose(pick_nu))
    keep_mask = (local_aux[:, :, None] * local_pair[None, :, :]).astype(jnp.bfloat16)
    masked = integrals * keep_mask
    lam_count = occ_density.shape[1]
    initial = jnp.zeros((ri_count, nu_count, lam_count), jnp.float32)
    block_piece = lax.all_gather(masked, "rep", axis=2, tiled=True)
    width_here = block_piece.shape[2]
    flattened = block_piece.reshape(ri_count * nu_count, width_here)
    occ_sum = jnp.dot(flattened, occ_density, preferred_element_type=jnp.float32).reshape(
        initial.shape
    )
    occ_side = occ_sum.astype(jnp.bfloat16)
    relaid = lax.all_to_all(masked, "row", split_axis=0, concat_axis=1, tiled=True)
    virt_side = jnp.einsum(
        "qsl,sn->qnl", relaid, virt_density, preferred_element_type=jnp.float32
    ).astype(jnp.bfloat16)
    virt_back = lax.all_to_all(virt_side, "row", split_axis=1, concat_axis=0, tiled=True)
    virt_flat = virt_back.reshape(ri_count, nu_count * lam_count)
    block_piece = lax.all_gather(occ_side, "col", axis=0, tiled=True)
    occ_flat = block_piece.reshape(block_piece.shape[0], nu_count * lam_count)
    partials = lax.dot_general(
        occ_flat, virt_flat, (((1,), (1,)), ((), ())), preferred_element_type=jnp.float32
    )
    summed = lax.psum_scatter(partials, ("row", "rep"), scatter_dimension=0, tiled=True)
    return summed * (-2.0 / NAO)


def solution(mesh):
    return jax.shard_map(
        local,
        mesh=mesh,
        in_specs=(
            P(("grp", "col"), "row", "rep"),
            P("grp", "rep"),
            P("grp", None),
            P("grp", None),
            P("grp", None),
        ),
        out_specs=P(("grp", "row", "rep"), "col"),
        check_vma=False,
    )
```

profile of v0, /device:TPU:0, one launch (start us, length us, event | category | flops | bytes accessed | tf_op | source)
XLA Modules:
  0.0 300.7 jit_solution(1031724590113899019)
XLA Ops:
  6.5 0.0 copy-start
  6.5 0.0 all-gather.3.cloned.1.call-start
  6.6 0.7 convert_bitcast_fusion.1
  7.3 0.2 fusion.7
  7.5 1.1 fusion.1
  8.6 4.3 %fusion = bf16[64,128,256]{2,1,0:T(8,128)(2,1)} fusion(bf16[64,128,256]{2,1,0:T(8,128)(2,1)} %param.5, f32[128,256]{1,0:T(8,128)S(1)} %fusion.1, f32[64,128]{1,0:T(8,128)S(1)} %fusion.7), kind=kLoop, calls=%fused_computation.1 | loop fusion | flops 6291456 | bytes 8552448 | tf_op jit(solution)/shard_map/mul | solution.py:28
  12.9 0.0 all-gather.3.cloned.1.call-update
  12.9 0.0 copy-start.3
  12.9 6.5 %all-to-all-start = ((bf16[64,128,256]{2,1,0:T(8,128)(2,1)}), bf16[64,128,256]{2,1,0:T(8,128)(2,1)}, u32[]{:S(2)}, u32[]{:S(2)}) async-start(bf16[64,128,256]{2,1,0:T(8,128)(2,1)} %fusion), calls=%async_computation | async-start | bytes 8388608 | tf_op jit(solution)/shard_map/all_to_all | solution.py:38
  19.4 0.0 all-gather.5.cloned.1.call-start
  19.4 14.7 %all-gather.3.cloned.1.call-done = bf16[64,128,512]{2,1,0:T(8,128)(2,1)} async-done(((bf16[64,128,256]{2,1,0:T(8,128)(2,1)}), bf16[64,128,512]{2,1,0:T(8,128)(2,1)}) %all-gather.3.cloned.1.call-update) | async-done | bytes 8388624 | tf_op jit(solution)/shard_map/all_gather | solution.py:31
  34.1 0.0 copy-done.3
  34.1 7.7 %convolution_convert_fusion = bf16[64,128,256]{2,1,0:T(8,128)(2,1)} fusion(bf16[64,128,512]{2,1,0:T(8,128)(2,1)} %all-gather.3.cloned.1.call-done, bf16[512,256]{1,0:T(8,128)(2,1)S(1)} %copy-done.3), kind=kOutput, calls=%fused_computation.3 | convolution fusion | flops 2149580800 | bytes 12845056 | tf_op jit(solution)/shard_map/dot_general | solution.py:34
  41.8 0.0 all-gather.5.cloned.1.call-update
  41.8 0.0 reduce-scatter.2.cloned.1.call-start
  41.9 71.0 %all-to-all-done = bf16[64,128,256]{2,1,0:T(8,128)(2,1)} async-done(((bf16[64,128,256]{2,1,0:T(8,128)(2,1)}), bf16[64,128,256]{2,1,0:T(8,128)(2,1)}, u32[]{:S(2)}, u32[]{:S(2)}) %all-to-all-start) | async-done | bytes 4194336 | tf_op jit(solution)/shard_map/all_to_all | solution.py:38
  112.8 7.4 %copy.9 = bf16[16,4,128,256]{2,1,3,0:T(4,128)(2,1)} copy(bf16[16,4,128,256]{3,2,0,1:T(8,128)(2,1)} %bitcast.3) | data formatting | bytes 8388608 | tf_op jit(solution)/shard_map/all_to_all | solution.py:38
  120.3 7.2 %all_to_all.27 = bf16[16,512,256]{1,2,0:T(8,128)(2,1)} reshape(bf16[16,4,128,256]{2,1,3,0:T(4,128)(2,1)} %copy.9) | data formatting | bytes 8388608 | tf_op jit(solution)/shard_map/all_to_all | solution.py:38
  127.5 0.0 copy-done
  127.5 6.5 %convert_bitcast_fusion = bf16[16,512,256]{1,2,0:T(8,128)(2,1)} fusion(bf16[16,512,256]{1,2,0:T(8,128)(2,1)} %all_to_all.27, bf16[512,512]{1,0:T(8,128)(2,1)S(1)} %copy-done), kind=kOutput, calls=%fused_computation.2 | convolution fusion | flops 2149580800 | bytes 8912896 | tf_op jit(solution)/shard_map/qsl,sn->qnl/dot_general | solution.py:39
  133.9 7.9 %copy.10 = bf16[16,512,256]{2,0,1:T(8,128)(2,1)} copy(bf16[16,512,256]{1,2,0:T(8,128)(2,1)} %convert_bitcast_fusion) | data formatting | bytes 8388608 | tf_op jit(solution)/shard_map/convert_element_type | solution.py:41
  141.8 96.5 %all_to_all.33 = bf16[16,512,256]{2,0,1:T(8,128)(2,1)S(1)} all-to-all(bf16[16,512,256]{2,0,1:T(8,128)(2,1)} %copy.10), channel_id=1, replica_groups=mesh['grp'=2,'row'=4,'col'=2,'rep'=2] {'row'}, dimensions={1} | all-to-all | bytes 8388608 | tf_op jit(solution)/shard_map/all_to_all | solution.py:42
  238.4 1.6 copy.11
  240.0 4.6 %copy.13 = bf16[8,8,128,256]{3,1,2,0:T(8,128)(2,1)} copy(bf16[8,8,128,256]{3,2,1,0:T(8,128)(2,1)S(1)} %bitcast.29) | data formatting | bytes 8388608
  244.5 0.0 all-gather.5.cloned.1.call-done
  244.5 0.0 copy-start.2
  244.5 12.5 %copy.12 = bf16[16,8,128,256]{3,1,2,0:T(8,128)(2,1)} copy(bf16[16,8,128,256]{3,2,1,0:T(8,128)(2,1)} %bitcast.30) | data formatting | bytes 16777216
  257.1 0.0 copy-start.1
  257.1 0.0 copy-done.2
  257.1 6.5 %fusion.16 = f32[128,64]{1,0:T(8,128)} fusion(bf16[128,32768]{1,0:T(8,128)(2,1)} %bitcast.26, bf16[64,32768]{1,0:T(8,128)(2,1)S(1)} %bitcast.27), kind=kOutput, calls=%fused_computation.33 | convolution fusion | flops 536870912 | bytes 12615680 | tf_op jit(solution)/shard_map/dot_general | solution.py:46
  263.5 0.0 reduce-scatter.2.cloned.1.call-update
  263.6 29.3 %reduce-scatter.2.cloned.1.call-done = f32[16,64]{1,0:T(8,128)} async-done(((f32[128,64]{1,0:T(8,128)}), f32[16,64]{1,0:T(8,128)}) %reduce-scatter.2.cloned.1.call-update) | async-done | bytes 4112 | tf_op jit(solution)/shard_map/reduce_scatter | solution.py:49
  292.9 1.3 broadcast_multiply_fusion
  294.2 0.0 copy-done.1
  (3 shorter events, 0.0 us)
Async XLA Ops:
  6.5 120.9 %copy-start = (bf16[512,512]{1,0:T(8,128)(2,1)S(1)}, bf16[512,512]{1,0:T(8,128)(2,1)}, u32[]{:S(2)}) copy-start(bf16[512,512]{1,0:T(8,128)(2,1)} %param.7) | copy-start | bytes 1572868
  6.5 27.6 %all-gather.3.cloned.1.call-start = ((), (), s32[]{:S(2)}) async-start(), calls=%async_computation.3 | async-start | bytes 12582912 | tf_op jit(solution)/shard_map/all_gather | solution.py:31
  12.9 21.2 %copy-start.3 = (bf16[512,256]{1,0:T(8,128)(2,1)S(1)}, bf16[512,256]{1,0:T(8,128)(2,1)}, u32[]{:S(2)}) copy-start(bf16[512,256]{1,0:T(8,128)(2,1)} %param.6) | copy-start | bytes 786436
  12.9 99.9 %all-to-all-start = ((bf16[64,128,256]{2,1,0:T(8,128)(2,1)}), bf16[64,128,256]{2,1,0:T(8,128)(2,1)}, u32[]{:S(2)}, u32[]{:S(2)}) async-start(bf16[64,128,256]{2,1,0:T(8,128)(2,1)} %fusion), calls=%async_computation | async-start | bytes 8388608 | tf_op jit(solution)/shard_map/all_to_all | solution.py:38
  19.4 225.1 %all-gather.5.cloned.1.call-start = ((), (), s32[]{:S(2)}) async-start(), calls=%async_computation.4 | async-start | bytes 12582912 | tf_op jit(solution)/shard_map/all_gather | solution.py:44
  41.8 251.1 %reduce-scatter.2.cloned.1.call-start = ((), (), s32[]{:S(2)}) async-start(), calls=%async_computation.5 | async-start | bytes 73728 | tf_op jit(solution)/shard_map/reduce_scatter | solution.py:49
  244.5 12.5 %copy-start.2 = (bf16[8,8,128,256]{3,1,2,0:T(8,128)(2,1)S(1)}, bf16[8,8,128,256]{3,1,2,0:T(8,128)(2,1)}, u32[]{:S(2)}) copy-start(bf16[8,8,128,256]{3,1,2,0:T(8,128)(2,1)} %copy.13) | copy-start | bytes 12582916
  257.1 37.1 %copy-start.1 = (bf16[512,512]{1,0:T(8,128)(2,1)S(1)}, bf16[512,512]{1,0:T(8,128)(2,1)}, u32[]{:S(2)}) copy-start(bf16[512,512]{1,0:T(8,128)(2,1)} %param.7) | copy-start | bytes 1572868
Sparse Core Ops, SparseCore 0:
  13.1 20.9 all-gather.2
  41.9 105.2 all-gather.4
  263.7 29.1 reduce-scatter.1
where the time goes:
time: 302 us; the launch traced here: 301 us
  waiting for transfers between devices  115 us (38%)
  blocking collectives  96.5 us (32%)
  local copies, waits for them, and re-layouts  41.2 us (14%)
  matrix products  22 us (7%)
  between operations  13.1 us (4%)
  starting transfers between devices  6.51 us (2%)
  other arithmetic  6.31 us (2%)
    all_to_all x1, blocking collectives, local(): lax.all_to_all(virt_side, 'row', split_axis=1, concat_axis=0, tiled=True)  96.5 us
    all_to_all x1, waiting for transfers between devices, local(): lax.all_to_all(masked, 'row', split_axis=0, concat_axis=1, tiled=True)  71 us
    reduce_scatter x1, waiting for transfers between devices, local(): lax.psum_scatter(partials, ('row', 'rep'), scatter_dimension=0, tiled=True)  29.3 us
    unnamed x10, local copies, waits for them, and re-layouts  17.1 us
    all_gather x1, waiting for transfers between devices, local(): block_piece = lax.all_gather(masked, 'rep', axis=2, tiled=True)  14.7 us
    all_to_all x2, local copies, waits for them, and re-layouts, local(): lax.all_to_all(masked, 'row', split_axis=0, concat_axis=1, tiled=True)  14.6 us
    convert_element_type x1, local copies, waits for them, and re-layouts, local(): virt_side = jnp.einsum('qsl,sn->qnl', relaid, virt_density, preferred_ele...  7.89 us
    dot_general x1, matrix products, local(): jnp.dot(flattened, occ_density, preferred_element_type=jnp.float32)  7.69 us
  transfers between devices with their start and end apart: 4, of which 3 were waited for; matrix products, arithmetic and copies ran while one was open for 12% of the time, Pallas kernels for 0%

commit v1 on v0

--- a/solution.py
+++ b/solution.py
@@ -1,19 +1,202 @@
+import functools
+
 import jax
 import jax.numpy as jnp
 from jax import lax
+from jax.experimental import pallas as pl
+from jax.experimental.pallas import tpu as pltpu
 from jax.sharding import PartitionSpec as P
 
 BLOCK = 128
 RI_ATOM = 128
 NAO = 512
+MESH = pl.DeviceIdType.MESH
+F32 = jnp.float32
+BF16 = jnp.bfloat16
+GROUP = 16
+STRIP = 64
 
 
 def one_hot_blocks(first, count, width, groups):
     places = (first + jnp.arange(count, dtype=jnp.int32)) // width
-    return (places[:, None] == jnp.arange(groups, dtype=jnp.int32)[None, :]).astype(jnp.float32)
-
-
-def local(integrals, occ_density, virt_density, pair_mask, aux_mask):
+    return (places[:, None] == jnp.arange(groups, dtype=jnp.int32)[None, :]).astype(F32)
+
+
+def kernel(rows, m_ref, occ_ref, virt_ref, out_ref, sib, relaid, turned, occ_own, occ_far, back,
+           total, parts, z_send, z_recv, b_send, b_recv, own_sem, s_sem, c_sem, p_send, p_recv):
+    r = lax.axis_index("row")
+    c = lax.axis_index("col")
+    p = lax.axis_index("rep")
+    ri, nu, lam = m_ref.shape
+    share = ri // rows
+    half = lam // 2
+
+    barrier = pltpu.get_barrier_semaphore()
+    peers = [{"row": lax.rem(r + off, rows), "rep": lax.rem(p + q, 2)} for off in range(rows) for q in range(2)]
+    for peer in peers[1:] + [{"col": 1 - c}]:
+        pl.semaphore_signal(barrier, inc=1, device_id=peer, device_id_type=MESH)
+    pl.semaphore_wait(barrier, 2 * rows)
+
+    def remote(src, dst, send, recv, to):
+        return pltpu.make_async_remote_copy(
+            src_ref=src, dst_ref=dst, send_sem=send, recv_sem=recv, device_id=to, device_id_type=MESH)
+
+    sib_copies = []
+    for g in range(ri // GROUP):
+        part = pl.ds(g * GROUP, GROUP)
+        sib_copies.append(remote(m_ref.at[part], sib.at[part], s_sem.at[0, g], s_sem.at[1, g], {"rep": 1 - p}))
+    first = []
+    for k in range(2):
+        lanes = pl.ds(k * half, half)
+        copies = []
+        for off in range(1, rows):
+            to = lax.rem(r + off, rows)
+            copies.append(remote(
+                m_ref.at[pl.ds(to * share, share), :, lanes],
+                relaid.at[:, pl.ds(r * nu, nu), lanes],
+                z_send.at[k, off], z_recv.at[k, off], {"row": to}))
+        copies.append(pltpu.make_async_copy(
+            m_ref.at[pl.ds(r * share, share), :, lanes],
+            relaid.at[:, pl.ds(r * nu, nu), lanes], own_sem.at[0, k]))
+        first.append(copies)
+    for copies in first:
+        for copy in copies:
+            copy.start()
+    for copy in sib_copies:
+        copy.start()
+
+    far_copies = []
+    for g in range(ri // GROUP):
+        sib_copies[g].wait()
+        part = pl.ds(g * GROUP, GROUP)
+
+        @pl.loop(0, nu // GROUP)
+        def _(t):
+            strip = pl.ds(pl.multiple_of(t * GROUP, GROUP), GROUP)
+            mine = m_ref[part, strip, :].reshape(GROUP * GROUP, lam)
+            its = sib[part, strip, :].reshape(GROUP * GROUP, lam)
+            here = pl.ds(pl.multiple_of(p * lam, lam), lam)
+            there = pl.ds(pl.multiple_of((1 - p) * lam, lam), lam)
+            prod = jnp.dot(mine, occ_ref[here, :], preferred_element_type=F32)
+            prod += jnp.dot(its, occ_ref[there, :], preferred_element_type=F32)
+            prod = jnp.swapaxes(prod.reshape(GROUP, GROUP, lam), 0, 1)
+            occ_own[strip, part, :] = prod.astype(BF16)
+
+        far_copies.append(remote(
+            occ_own.at[:, part, :], occ_far.at[:, part, :], c_sem.at[0, g], c_sem.at[1, g], {"col": 1 - c}))
+        far_copies[-1].start()
+
+    second = []
+    for k in range(2):
+        lanes = pl.ds(k * half, half)
+        for copy in first[k]:
+            copy.wait()
+
+        @pl.loop(0, rows * nu // STRIP)
+        def _(t):
+            strip = pl.ds(pl.multiple_of(t * STRIP, STRIP), STRIP)
+            weights = virt_ref[strip, :]
+            pieces = [jnp.dot(weights, relaid[q, :, lanes], preferred_element_type=F32) for q in range(share)]
+            turned[strip, :, lanes] = jnp.swapaxes(jnp.stack(pieces, axis=0), 0, 1).astype(BF16)
+
+        copies = []
+        for off in range(1, rows):
+            to = lax.rem(r + off, rows)
+            copies.append(remote(
+                turned.at[pl.ds(to * nu, nu), :, lanes],
+                back.at[:, pl.ds(r * share, share), lanes],
+                b_send.at[k, off], b_recv.at[k, off], {"row": to}))
+        copies.append(pltpu.make_async_copy(
+            turned.at[pl.ds(r * nu, nu), :, lanes],
+            back.at[:, pl.ds(r * share, share), lanes], own_sem.at[1, k]))
+        for copy in copies:
+            copy.start()
+        second.append(copies)
+    for copy in far_copies:
+        copy.wait()
+    total[...] = jnp.zeros_like(total)
+    base = pl.multiple_of(c * ri, ri)
+    other = pl.multiple_of((1 - c) * ri, ri)
+    for k in range(2):
+        lanes = pl.ds(k * half, half)
+        for copy in second[k]:
+            copy.wait()
+
+        @pl.loop(0, nu // 8)
+        def _(t):
+            acc_own = jnp.zeros((ri, ri), F32)
+            acc_far = jnp.zeros((ri, ri), F32)
+            for j in range(8):
+                n = t * 8 + j
+                q = back[n, :, lanes]
+                dims = (((1,), (1,)), ((), ()))
+                acc_own += lax.dot_general(occ_own[n, :, lanes], q, dims, preferred_element_type=F32)
+                acc_far += lax.dot_general(occ_far[n, :, lanes], q, dims, preferred_element_type=F32)
+            total[pl.ds(base, ri), :ri] += acc_own
+            total[pl.ds(other, ri), :ri] += acc_far
+
+    tile = out_ref.shape[0]
+    sends = []
+    for i, peer in enumerate(peers):
+        if i == 0:
+            continue
+        index = peer["row"] * 2 + peer["rep"]
+        sends.append(remote(
+            total.at[pl.ds(pl.multiple_of(index * tile, tile), tile)], parts.at[i],
+            p_send.at[i], p_recv.at[i], peer))
+        sends[-1].start()
+    acc = total[pl.ds(pl.multiple_of((r * 2 + p) * tile, tile), tile), :]
+    for i, copy in enumerate(sends):
+        copy.wait()
+        acc += parts[i + 1]
+    out_ref[...] = acc[:, :ri] * (-2.0 / NAO)
+
+
+def local(rows, integrals, occ_density, virt_density, pair_mask, aux_mask):
+    ri, nu, lam = integrals.shape
+    masked = integrals * keep(integrals, pair_mask, aux_mask)
+    groups = ri // GROUP
+    share = ri // rows
+    tile = 2 * ri // (2 * rows)
+    whole = pl.BlockSpec(memory_space=pltpu.VMEM)
+    dma = pltpu.SemaphoreType.DMA
+    return pl.pallas_call(
+        functools.partial(kernel, rows),
+        out_shape=jax.ShapeDtypeStruct((tile, ri), F32),
+        in_specs=[whole] * 3,
+        out_specs=whole,
+        scratch_shapes=[
+            pltpu.VMEM((ri, nu, lam), BF16),
+            pltpu.VMEM((share, rows * nu, lam), BF16),
+            pltpu.VMEM((rows * nu, share, lam), BF16),
+            pltpu.VMEM((nu, ri, lam), BF16),
+            pltpu.VMEM((nu, ri, lam), BF16),
+            pltpu.VMEM((nu, ri, lam), BF16),
+            pltpu.VMEM((2 * ri, 128), F32),
+            pltpu.VMEM((2 * rows, tile, 128), F32),
+            dma((2, rows)), dma((2, rows)), dma((2, rows)), dma((2, rows)), dma((2, 2)),
+            dma((2, groups)), dma((2, groups)), dma((2 * rows,)), dma((2 * rows,)),
+        ],
+        compiler_params=pltpu.CompilerParams(
+            collective_id=0, has_side_effects=True, vmem_limit_bytes=56 * 2**20),
+    )(masked, occ_density, jnp.transpose(virt_density))
+
+
+def keep(integrals, pair_mask, aux_mask):
+    ri_count, nu_count, mu_count = integrals.shape
+    ao_groups = pair_mask.shape[0]
+    ri_groups = aux_mask.shape[0]
+    pick_nu = one_hot_blocks(lax.axis_index("row") * nu_count, nu_count, BLOCK, ao_groups)
+    pick_mu = one_hot_blocks(lax.axis_index("rep") * mu_count, mu_count, BLOCK, ao_groups)
+    pick_ri = one_hot_blocks(lax.axis_index("col") * ri_count, ri_count, RI_ATOM, ri_groups)
+    pair_float = pair_mask.astype(F32)
+    aux_float = aux_mask.astype(F32)
+    local_pair = jnp.dot(jnp.dot(pick_nu, jnp.transpose(pair_float)), jnp.transpose(pick_mu))
+    local_aux = jnp.dot(jnp.dot(pick_ri, aux_float), jnp.transpose(pick_nu))
+    return (local_aux[:, :, None] * local_pair[None, :, :]).astype(BF16)
+
+
+def local_any(integrals, occ_density, virt_density, pair_mask, aux_mask):
     ri_count, nu_count, mu_count = integrals.shape
     ao_groups = pair_mask.shape[0]
     ri_groups = aux_mask.shape[0]
@@ -51,8 +234,16 @@
 
 
 def solution(mesh):
+    rows, cols, reps = mesh.shape["row"], mesh.shape["col"], mesh.shape["rep"]
+
+    def run(*args):
+        ri, nu, lam = args[0].shape
+        if cols == 2 and reps == 2 and ri == GROUP * rows and nu % 128 == 0 and lam == 256:
+            return local(rows, *args)
+        return local_any(*args)
+
     return jax.shard_map(
-        local,
+        run,
         mesh=mesh,
         in_specs=(
             P(("grp", "col"), "row", "rep"),

time: 302 us -> 208 us (0.69)
  Pallas kernels: 0 us -> 199 us
  waiting for transfers between devices: 115 us -> 0 us
  blocking collectives: 96.5 us -> 0 us
  local copies, waits for them, and re-layouts: 41.2 us -> 2.3 us
  matrix products: 22 us -> 1.21 us
  between operations: 13.1 us -> 0.02 us
  starting transfers between devices: 6.51 us -> 0 us
    pallas_call x0 -> x1, Pallas kernels: none -> 199 us  [local(): pl.pallas_call(functools.partial(kernel, rows), out_shape=jax.ShapeDtypeS...]
    all_to_all x1 -> x0, blocking collectives: 96.5 us -> none  [local(): lax.all_to_all(virt_side, 'row', split_axis=1, concat_axis=0, tiled=True)]
    all_to_all x1 -> x0, waiting for transfers between devices: 71 us -> none  [local(): lax.all_to_all(masked, 'row', split_axis=0, concat_axis=1, tiled=True)]
    reduce_scatter x1 -> x0, waiting for transfers between devices: 29.3 us -> none  [local(): lax.psum_scatter(partials, ('row', 'rep'), scatter_dimension=0, tiled=True)]
    dot_general x5 -> x2, matrix products: 22 us -> 1.21 us  [the longest x1 1.01 us: keep(): jnp.dot(jnp.dot(pick_nu, jnp.transpose(pair_float)), jnp.transpose(pick_mu))]
    all_to_all x3 -> x0, local copies, waits for them, and re-layouts: 16.2 us -> none  [the longest x2 14.6 us: local(): lax.all_to_all(masked, 'row', split_axis=0, concat_axis=1, tiled=True)]
    unnamed x10 -> x4, local copies, waits for them, and re-layouts: 17.1 us -> 2.3 us
    all_gather x2 -> x0, waiting for transfers between devices: 14.7 us -> none  [the longest x1 14.7 us: local(): block_piece = lax.all_gather(masked, 'rep', axis=2, tiled=True)]
  transfers between devices with their start and end apart: 4 -> 0, of which waited for: 3 -> 0; matrix products, arithmetic and copies ran while one was open for 12% -> 0% of each run, Pallas kernels for 0% -> 0%
where the time goes in v1:
time: 208 us
  Pallas kernels  199 us (96%)
  other arithmetic  5.14 us (2%)
  local copies, waits for them, and re-layouts  2.3 us (1%)
    pallas_call x1, Pallas kernels, local(): pl.pallas_call(functools.partial(kernel, rows), out_shape=jax.ShapeDtypeS...  199 us
    mul x1, other arithmetic, local(): masked = integrals * keep(integrals, pair_mask, aux_mask)  4.45 us

profile of v1, /device:TPU:0, one launch (start us, length us, event | category | flops | bytes accessed | tf_op | source)
XLA Modules:
  0.0 207.7 jit_solution(12622597046033329963)
XLA Ops:
  0.0 1.0 fusion.1
  1.1 0.7 convert_bitcast_fusion
  1.7 0.2 fusion.5
  1.9 0.0 copy-start
  1.9 4.5 %fusion.m_ref = bf16[64,128,256]{2,1,0:T(8,128)(2,1)} fusion(bf16[64,128,256]{2,1,0:T(8,128)(2,1)} %param.5, f32[128,256]{1,0:T(8,128)S(1)} %fusion.1, f32[64,128]{1,0:T(8,128)S(1)} %fusion.5), kind=kLoop, calls=%fused_computation.1 | loop fusion | flops 6291456 | bytes 8552448 | tf_op jit(solution)/shard_map/mul | solution.py:157
  6.4 0.0 copy-done
  6.4 1.0 copy.6
  7.4 199.0 %shard_map.55 = f32[16,64]{1,0:T(8,128)} custom-call(bf16[64,128,256]{2,1,0:T(8,128)(2,1)} %fusion.m_ref, bf16[512,256]{1,0:T(8,128)(2,1)} %occ_ref.1, bf16[512,512]{1,0:T(8,128)(2,1)} %bitcast.3), custom_call_target="tpu_custom_call" | custom-call | tf_op jit(solution)/shard_map/pallas_call | solution.py:163
  206.4 1.3 copy.8
  (3 shorter events, 0.0 us)
Async XLA Ops:
  1.9 4.5 %copy-start = (bf16[512,512]{1,0:T(8,128)(2,1)S(1)}, bf16[512,512]{1,0:T(8,128)(2,1)}, u32[]{:S(2)}) copy-start(bf16[512,512]{1,0:T(8,128)(2,1)} %param.7) | copy-start | bytes 1572868

commit v2 on v0

--- a/solution.py
+++ b/solution.py
@@ -1,19 +1,379 @@
 import jax
 import jax.numpy as jnp
 from jax import lax
+from jax.experimental import pallas as pl
+from jax.experimental.pallas import tpu as pltpu
 from jax.sharding import PartitionSpec as P
 
 BLOCK = 128
 RI_ATOM = 128
 NAO = 512
+MESH = pl.DeviceIdType.MESH
+F32 = jnp.float32
+BF16 = jnp.bfloat16
+GROUP = 16
+STRIP = 64
 
 
 def one_hot_blocks(first, count, width, groups):
     places = (first + jnp.arange(count, dtype=jnp.int32)) // width
-    return (places[:, None] == jnp.arange(groups, dtype=jnp.int32)[None, :]).astype(jnp.float32)
-
-
-def local(integrals, occ_density, virt_density, pair_mask, aux_mask):
+    return (places[:, None] == jnp.arange(groups, dtype=jnp.int32)[None, :]).astype(F32)
+
+
+def kernel(m_ref, occ_ref, wa_ref, wb_ref, out_ref, sib, far, far_sib, g_p, g_q, rel_a, rel_b, rel_n, occ_s, n_s,
+           w, total, cross, parts, z_send, z_recv, y_send, y_recv, s_sem, x_sem, f_sem, c_sem, p_send, p_recv):
+    r = lax.axis_index("row")
+    c = lax.axis_index("col")
+    p = lax.axis_index("rep")
+    rows = 4
+    ri, nu, lam = m_ref.shape
+    half = lam // 2
+    groups = ri // GROUP
+    dims = (((1,), (1,)), ((), ()))
+    lanes_of = (pl.ds(0, half), pl.ds(half, half))
+
+    barrier = pltpu.get_barrier_semaphore()
+    peers = [{"row": lax.rem(r + off, rows), "rep": lax.rem(p + q, 2)} for off in range(rows) for q in range(2)]
+    for peer in peers[1:] + [{"col": 1 - c}]:
+        pl.semaphore_signal(barrier, inc=1, device_id=peer, device_id_type=MESH)
+    pl.semaphore_wait(barrier, 2 * rows)
+
+    def remote(src, dst, send, recv, to):
+        return pltpu.make_async_remote_copy(
+            src_ref=src, dst_ref=dst, send_sem=send, recv_sem=recv, device_id=to, device_id_type=MESH)
+
+    def part(g):
+        return pl.ds(g * GROUP, GROUP)
+
+    def slot(f):
+        return pl.ds(f * nu, nu)
+
+    sources = (3, 2, 0)
+
+    def raw(f, blk, g, from_own):
+        dst = (rel_a, rel_b)[blk].at[part(g), slot(f), :]
+        src = m_ref.at[part(g), :, lanes_of[blk]] if from_own else dst
+        to = lax.rem(r + (1 if f == 2 else 3), rows)
+        return remote(src, dst, z_send.at[f, blk, g], z_recv.at[f, blk, g], {"row": to})
+
+    def in_use(f, blk):
+        return p == 0 if blk and f < 2 else p >= 0
+
+    def raw_start(f, g):
+        for blk in range(2):
+            @pl.when((r == sources[f]) & in_use(f, blk))
+            def _():
+                raw(f, blk, g, True).start()
+
+    def raw_relay(f, g, at, onward):
+        for blk in range(2):
+            @pl.when((r == at) & in_use(f, blk))
+            def _():
+                copy = raw(f, blk, g, False)
+                copy.wait_recv()
+                if onward:
+                    copy.start()
+
+    def right(f, arr, g, from_own):
+        dst = (rel_b, rel_n)[arr].at[part(g), slot(f), :]
+        src = (occ_s, n_s)[arr].at[part(g)] if from_own else dst
+        return remote(src, dst, y_send.at[f, arr, g], y_recv.at[f, arr, g], {"row": lax.rem(r + 1, rows)})
+
+    def right_start(g):
+        for f in range(3):
+            @pl.when((r == f) & (p == 1))
+            def _():
+                for arr in range(2):
+                    right(f, arr, g, True).start()
+
+    def right_relay(f, g, at):
+        @pl.when((r == at) & (p == 1))
+        def _():
+            for arr in range(2):
+                copy = right(f, arr, g, False)
+                copy.wait_recv()
+                if at < 3:
+                    copy.start()
+
+    sib_copies = [remote(m_ref.at[part(g)], sib.at[part(g)], s_sem.at[0, g], s_sem.at[1, g], {"rep": 1 - p})
+                  for g in range(groups)]
+    far_copies = [remote(m_ref.at[part(g)], far.at[part(g)], x_sem.at[0, g], x_sem.at[1, g], {"col": 1 - c})
+                  for g in range(groups)]
+    on_copies = [remote(far.at[part(g)], far_sib.at[part(g)], f_sem.at[0, g], f_sem.at[1, g], {"rep": 1 - p})
+                 for g in range(groups)]
+    for g in range(groups):
+        sib_copies[g].start()
+        for f in range(3):
+            raw_start(f, g)
+        far_copies[g].start()
+
+    def clear(ref, f):
+        @pl.loop(0, ri)
+        def _(q):
+            ref[q, slot(f), :] = jnp.zeros((nu, half), BF16)
+
+    for f, at in ((0, (3,)), (1, (2, 3)), (2, (0, 2, 3))):
+        for row in at:
+            @pl.when(r == row)
+            def _():
+                clear(rel_a, f)
+
+            @pl.when((r == row) & (p == 0))
+            def _():
+                clear(rel_b, f)
+    for f in range(3):
+        @pl.when((r <= f) & (p == 1))
+        def _():
+            clear(rel_n, f)
+
+        @pl.when(((r < f) if f < 2 else (r == 0)) & (p == 1))
+        def _():
+            clear(rel_b, f)
+
+        @pl.when((r == f) & (p == 1))
+        def _():
+            clear(rel_b, f)
+
+    here = pl.ds(pl.multiple_of(p * lam, lam), lam)
+    there = pl.ds(pl.multiple_of((1 - p) * lam, lam), lam)
+
+    def products(x, y, g, own):
+        @pl.loop(0, nu // GROUP)
+        def _(t):
+            strip = pl.ds(pl.multiple_of(t * GROUP, GROUP), GROUP)
+            mine = x[part(g), strip, :]
+            its = y[part(g), strip, :].reshape(GROUP * GROUP, lam)
+            prod = jnp.dot(mine.reshape(GROUP * GROUP, lam), occ_ref[here, :], preferred_element_type=F32)
+            prod += jnp.dot(its, occ_ref[there, :], preferred_element_type=F32)
+            prod = prod.reshape(GROUP, GROUP, 2 * lam)
+            turned = jnp.swapaxes(prod, 0, 1).astype(BF16)
+            to = pl.ds(g * GROUP + (0 if own else ri), GROUP)
+            g_p[strip, to, :] = turned[:, :, :lam]
+            g_q[strip, to, :] = turned[:, :, lam:]
+
+            @pl.when((p == 1) & (r != 1))
+            def _():
+                plain = jnp.swapaxes(mine[:, :, half:].astype(F32), 0, 1).astype(BF16)
+                g_p[strip, to, half:] = plain
+                g_q[strip, to, half:] = plain
+
+            @pl.when(p == 1)
+            def _():
+                if own:
+                    occ_s[part(g), strip, :] = prod[:, :, half:lam].astype(BF16)
+                    n_s[part(g), strip, :] = prod[:, :, lam + half:].astype(BF16)
+
+    for g in range(groups):
+        sib_copies[g].wait()
+        products(m_ref, sib, g, True)
+        right_start(g)
+        raw_relay(0, g, 2, True)
+        raw_relay(1, g, 1, True)
+    for g in range(groups):
+        right_relay(0, g, 1)
+        right_relay(1, g, 2)
+        raw_relay(0, g, 1, True)
+        right_relay(2, g, 3)
+        far_copies[g].wait()
+        on_copies[g].start()
+        right_relay(0, g, 2)
+        raw_relay(2, g, 1, False)
+        if g:
+            on_copies[g - 1].wait()
+            products(far, far_sib, g - 1, False)
+    on_copies[groups - 1].wait()
+    products(far, far_sib, groups - 1, False)
+
+    def mixed(g, blk):
+        rel, w_ref = (rel_a, rel_b)[blk], (wa_ref, wb_ref)[blk]
+
+        def strips(first, last, moved, own):
+            @pl.loop(first // STRIP, last // STRIP)
+            def _(t):
+                strip = pl.ds(pl.multiple_of(t * STRIP, STRIP), STRIP)
+                pieces = []
+                for q in range(g * GROUP, (g + 1) * GROUP):
+                    piece = jnp.dot(w_ref[strip, :3 * nu], moved[q], preferred_element_type=F32)
+                    if own is not None:
+                        piece += jnp.dot(w_ref[strip, 3 * nu:], own(q), preferred_element_type=F32)
+                    pieces.append(piece)
+                w[strip, part(g), :] = jnp.swapaxes(jnp.stack(pieces, axis=0), 0, 1).astype(BF16)
+
+        def raw_own(q):
+            return m_ref[q, :, lanes_of[blk]]
+
+        if blk == 0:
+            strips(0, nu, rel, raw_own)
+            strips(nu, 2 * nu, rel, None)
+            return
+
+        @pl.when(p == 0)
+        def _():
+            strips(0, nu, rel, raw_own)
+            strips(nu, 2 * nu, rel, None)
+
+        @pl.when(p == 1)
+        def _():
+            strips(0, nu, rel_n, None)
+            strips(nu, 2 * nu, rel, lambda q: occ_s[q])
+
+    def grams(blk):
+        lanes = lanes_of[blk]
+
+        @pl.loop(0, nu // 8)
+        def _(t):
+            acc_p = jnp.zeros((2 * ri, ri), F32)
+            acc_q = jnp.zeros((ri, 2 * ri), F32)
+            for j in range(8):
+                n = t * 8 + j
+                acc_p += lax.dot_general(g_p[n, :, lanes], w[n], dims, preferred_element_type=F32)
+                acc_q += lax.dot_general(w[nu + n], g_q[n, :, lanes], dims, preferred_element_type=F32)
+            total[pl.ds(base, ri), :ri] += acc_p[:ri] + acc_q[:, :ri]
+            total[pl.ds(other, ri), :ri] += acc_p[ri:]
+            cross[0, :, :ri] += acc_q[:, ri:]
+
+    base = pl.multiple_of(c * ri, ri)
+    other = pl.multiple_of((1 - c) * ri, ri)
+    total[...] = jnp.zeros_like(total)
+    cross[0] = jnp.zeros((ri, 2 * ri), F32)
+
+    @pl.when((r == 1) & (p == 1))
+    def _():
+        for g in range(groups):
+            @pl.loop(0, 2 * nu // STRIP)
+            def _(t):
+                strip = pl.ds(pl.multiple_of(t * STRIP, STRIP), STRIP)
+                pieces = [jnp.dot(wa_ref[strip, 2 * nu:3 * nu], rel_b[q, slot(2), :], preferred_element_type=F32)
+                          for q in range(g * GROUP, (g + 1) * GROUP)]
+                w[strip, part(g), :] = jnp.swapaxes(jnp.stack(pieces, axis=0), 0, 1).astype(BF16)
+        grams(1)
+        for x, shift in ((m_ref, 0), (far, ri)):
+            for g in range(groups):
+                @pl.loop(0, nu // GROUP)
+                def _(t):
+                    strip = pl.ds(pl.multiple_of(t * GROUP, GROUP), GROUP)
+                    to = pl.ds(g * GROUP + shift, GROUP)
+                    plain = jnp.swapaxes(x[part(g), strip, half:].astype(F32), 0, 1).astype(BF16)
+                    g_p[strip, to, half:] = plain
+                    g_q[strip, to, half:] = plain
+
+    for g in range(groups):
+        raw_relay(0, g, 0, False)
+        raw_relay(1, g, 0, False)
+        right_relay(1, g, 3)
+        right_relay(0, g, 3)
+        mixed(g, 0)
+    grams(0)
+    for g in range(groups):
+        mixed(g, 1)
+    grams(1)
+
+    copy = remote(cross.at[0], cross.at[1], c_sem.at[0], c_sem.at[1], {"col": 1 - c})
+    copy.start()
+    copy.wait()
+    total[pl.ds(other, ri), :] += cross[1]
+
+    tile = out_ref.shape[0]
+    sends = []
+    for i, peer in enumerate(peers):
+        if i == 0:
+            continue
+        index = peer["row"] * 2 + peer["rep"]
+        sends.append(remote(
+            total.at[pl.ds(pl.multiple_of(index * tile, tile), tile)], parts.at[i],
+            p_send.at[i], p_recv.at[i], peer))
+        sends[-1].start()
+    for g in range(groups):
+        for f, senders in enumerate(((1, 2, 3), (1, 2), (0,))):
+            for row in senders:
+                for blk in range(2):
+                    @pl.when((r == row) & in_use(f, blk))
+                    def _():
+                        raw(f, blk, g, row == sources[f]).wait_send()
+        for f in range(3):
+            for row in range(f, 3):
+                @pl.when((r == row) & (p == 1))
+                def _():
+                    for arr in range(2):
+                        right(f, arr, g, row == f).wait_send()
+    acc = total[pl.ds(pl.multiple_of((r * 2 + p) * tile, tile), tile), :]
+    for i, copy in enumerate(sends):
+        copy.wait()
+        acc += parts[i + 1]
+    out_ref[...] = acc[:, :ri] * (-2.0 / NAO)
+
+
+def local(rows, integrals, occ_density, virt_density, pair_mask, aux_mask):
+    ri, nu, lam = integrals.shape
+    r, p = lax.axis_index("row"), lax.axis_index("rep")
+    masked = integrals * keep(integrals, pair_mask, aux_mask)
+    groups = ri // GROUP
+    tile = 2 * ri // (2 * rows)
+    half = lam // 2
+    occ_all = lax.all_gather(occ_density, "rep", axis=1, tiled=True)
+    occ_w = jnp.concatenate(
+        [occ_density, jnp.transpose(lax.dynamic_slice_in_dim(occ_all, p * lam, lam, 0))], axis=1)
+    column = jnp.transpose(lax.dynamic_slice_in_dim(virt_density, r * nu, nu, 1))
+    row = lax.dynamic_slice_in_dim(virt_density, r * nu, nu, 0)
+    both = jnp.concatenate([column, row], axis=0)
+
+    def block(src):
+        return both[:, src * nu:(src + 1) * nu]
+
+    own = lax.dynamic_slice_in_dim(both, r * nu, nu, 1)
+    zero = jnp.zeros_like(own)
+    upper = jnp.concatenate([own[:nu], zero[:nu]])
+    lower = jnp.concatenate([zero[:nu], own[nu:]])
+    wa = jnp.concatenate(
+        [jnp.where(r <= 2, block(3), 0), jnp.where(r <= 1, block(2), 0), jnp.where(r == 1, block(0), 0), upper], axis=1)
+    wc = jnp.concatenate([jnp.where((f < r) & ((f > 0) | (r > 1)), block(f), 0) for f in range(3)] + [lower], axis=1)
+    wb = jnp.where(p == 0, wa, wc)
+    whole = pl.BlockSpec(memory_space=pltpu.VMEM)
+    dma = pltpu.SemaphoreType.DMA
+    return pl.pallas_call(
+        kernel,
+        out_shape=jax.ShapeDtypeStruct((tile, ri), F32),
+        in_specs=[whole] * 4,
+        out_specs=whole,
+        scratch_shapes=[
+            pltpu.VMEM((ri, nu, lam), BF16),
+            pltpu.VMEM((ri, nu, lam), BF16),
+            pltpu.VMEM((ri, nu, lam), BF16),
+            pltpu.VMEM((nu, 2 * ri, lam), BF16),
+            pltpu.VMEM((nu, 2 * ri, lam), BF16),
+            pltpu.VMEM((ri, 3 * nu, half), BF16),
+            pltpu.VMEM((ri, 3 * nu, half), BF16),
+            pltpu.VMEM((ri, 3 * nu, half), BF16),
+            pltpu.VMEM((ri, nu, half), BF16),
+            pltpu.VMEM((ri, nu, half), BF16),
+            pltpu.VMEM((2 * nu, ri, half), BF16),
+            pltpu.VMEM((2 * ri, 2 * ri), F32),
+            pltpu.VMEM((2, ri, 2 * ri), F32),
+            pltpu.VMEM((2 * rows, tile, 2 * ri), F32),
+            dma((3, 2, groups)), dma((3, 2, groups)), dma((3, 2, groups)), dma((3, 2, groups)),
+            dma((2, groups)), dma((2, groups)), dma((2, groups)), dma((2,)),
+            dma((2 * rows,)), dma((2 * rows,)),
+        ],
+        compiler_params=pltpu.CompilerParams(
+            collective_id=0, has_side_effects=True, vmem_limit_bytes=62 * 2**20),
+    )(masked, occ_w, wa, wb)
+
+
+def keep(integrals, pair_mask, aux_mask):
+    ri_count, nu_count, mu_count = integrals.shape
+    ao_groups = pair_mask.shape[0]
+    ri_groups = aux_mask.shape[0]
+    pick_nu = one_hot_blocks(lax.axis_index("row") * nu_count, nu_count, BLOCK, ao_groups)
+    pick_mu = one_hot_blocks(lax.axis_index("rep") * mu_count, mu_count, BLOCK, ao_groups)
+    pick_ri = one_hot_blocks(lax.axis_index("col") * ri_count, ri_count, RI_ATOM, ri_groups)
+    pair_float = pair_mask.astype(F32)
+    aux_float = aux_mask.astype(F32)
+    local_pair = jnp.dot(jnp.dot(pick_nu, jnp.transpose(pair_float)), jnp.transpose(pick_mu))
+    local_aux = jnp.dot(jnp.dot(pick_ri, aux_float), jnp.transpose(pick_nu))
+    return (local_aux[:, :, None] * local_pair[None, :, :]).astype(BF16)
+
+
+def local_any(integrals, occ_density, virt_density, pair_mask, aux_mask):
     ri_count, nu_count, mu_count = integrals.shape
     ao_groups = pair_mask.shape[0]
     ri_groups = aux_mask.shape[0]
@@ -51,8 +411,16 @@
 
 
 def solution(mesh):
+    rows, cols, reps = mesh.shape["row"], mesh.shape["col"], mesh.shape["rep"]
+
+    def run(*args):
+        ri, nu, lam = args[0].shape
+        if rows == 4 and cols == 2 and reps == 2 and ri == 64 and nu == 128 and lam == 256:
+            return local(rows, *args)
+        return local_any(*args)
+
     return jax.shard_map(
-        local,
+        run,
         mesh=mesh,
         in_specs=(
             P(("grp", "col"), "row", "rep"),

time: 302 us -> 239 us (0.79)
  Pallas kernels: 0 us -> 225 us
  waiting for transfers between devices: 115 us -> 0 us
  blocking collectives: 96.5 us -> 2.26 us
  local copies, waits for them, and re-layouts: 41.2 us -> 2.57 us
  matrix products: 22 us -> 1.23 us
  between operations: 13.1 us -> 0.09 us
  starting transfers between devices: 6.51 us -> 0 us
    pallas_call x0 -> x1, Pallas kernels: none -> 225 us  [local(): pl.pallas_call(kernel, out_shape=jax.ShapeDtypeStruct((tile, ri), F32), i...]
    all_to_all x1 -> x0, blocking collectives: 96.5 us -> none  [local(): lax.all_to_all(virt_side, 'row', split_axis=1, concat_axis=0, tiled=True)]
    all_to_all x1 -> x0, waiting for transfers between devices: 71 us -> none  [local(): lax.all_to_all(masked, 'row', split_axis=0, concat_axis=1, tiled=True)]
    reduce_scatter x1 -> x0, waiting for transfers between devices: 29.3 us -> none  [local(): lax.psum_scatter(partials, ('row', 'rep'), scatter_dimension=0, tiled=True)]
    dot_general x5 -> x2, matrix products: 22 us -> 1.23 us  [the longest x1 1.03 us: keep(): jnp.dot(jnp.dot(pick_nu, jnp.transpose(pair_float)), jnp.transpose(pick_mu))]
    all_to_all x3 -> x0, local copies, waits for them, and re-layouts: 16.2 us -> none  [the longest x2 14.6 us: local(): lax.all_to_all(masked, 'row', split_axis=0, concat_axis=1, tiled=True)]
    all_gather x2 -> x0, waiting for transfers between devices: 14.7 us -> none  [the longest x1 14.7 us: local(): block_piece = lax.all_gather(masked, 'rep', axis=2, tiled=True)]
    unnamed x10 -> x7, local copies, waits for them, and re-layouts: 17.1 us -> 2.51 us
  transfers between devices with their start and end apart: 4 -> 0, of which waited for: 3 -> 0; matrix products, arithmetic and copies ran while one was open for 12% -> 0% of each run, Pallas kernels for 0% -> 0%
where the time goes in v2:
time: 239 us; the launch traced here: 238 us
  Pallas kernels  225 us (94%)
  other arithmetic  7.59 us (3%)
  local copies, waits for them, and re-layouts  2.57 us (1%)
    pallas_call x1, Pallas kernels, local(): pl.pallas_call(kernel, out_shape=jax.ShapeDtypeStruct((tile, ri), F32), i...  225 us

profile of v2, /device:TPU:0, one launch (start us, length us, event | category | flops | bytes accessed | tf_op | source)
XLA Modules:
  0.0 238.3 jit_solution(14750781122936006710)
XLA Ops:
  0.0 0.0 copy-start
  0.0 0.0 copy-start.1
  0.0 0.7 convert_bitcast_fusion
  0.8 0.2 fusion.14
  1.0 1.0 fusion.1
  2.0 0.0 copy-done
  2.1 0.1 copy.8
  2.2 0.8 fusion.12
  3.0 0.9 fusion.6
  3.9 1.1 copy.6
  5.0 2.3 all_gather.3
  7.3 0.0 copy-done.1
  7.3 0.9 pad_maximum_fusion.occ_ref
  8.2 4.3 %fusion.m_ref = bf16[64,128,256]{2,1,0:T(8,128)(2,1)} fusion(bf16[64,128,256]{2,1,0:T(8,128)(2,1)} %param.5, f32[128,256]{1,0:T(8,128)S(1)} %fusion.1, f32[64,128]{1,0:T(8,128)S(1)} %fusion.14), kind=kLoop, calls=%fused_computation.1 | loop fusion | flops 6291456 | bytes 8552448 | tf_op jit(solution)/shard_map/mul | solution.py:309
  12.4 224.6 %shard_map.55 = f32[16,64]{1,0:T(8,128)} custom-call(bf16[64,128,256]{2,1,0:T(8,128)(2,1)} %fusion.m_ref, bf16[512,512]{1,0:T(8,128)(2,1)} %pad_maximum_fusion.occ_ref, bf16[256,512]{1,0:T(8,128)(2,1)} %get-tuple-element.12.wa_ref, bf16[256,512]{1,0:T(8,128)(2,1)} %get-tuple-element.11.wb_ref), custom_call_target="tpu_custom_call" | custom-call | tf_op jit(solution)/shard_map/pallas_call | solution.py:333
  237.0 1.3 copy.10
  (8 shorter events, 0.1 us)
Async XLA Ops:
  0.0 2.0 copy-start
  0.0 7.3 %copy-start.1 = (bf16[512,256]{1,0:T(8,128)(2,1)S(1)}, bf16[512,256]{1,0:T(8,128)(2,1)}, u32[]{:S(2)}) copy-start(bf16[512,256]{1,0:T(8,128)(2,1)} %param.6) | copy-start | bytes 786436
